TPU v7x, 32 devices: a whole 2x2x4 slice. The times are simulated.
32 devices in a mesh: row: 8 (over z, x), col: 4 (over y, core).
Axes of the slice: x: 2, y: 2, z: 4, core: 2. Of those that a mesh axis runs over, the one named last changes fastest.
Arguments:
- pixels: bfloat16 [128, 64, 768], P('row', 'col'), may hold values from -6 to 6
- conv_weight: bfloat16 [3, 3, 64, 128], replicated, may hold values from -0.25 to 0.25
- time_weight: bfloat16 [3, 16, 8, 8], replicated, may hold values from -1.25 to 1.25
- class_weight: bfloat16 [128, 20], replicated, may hold values from -0.5 to 0.5
- pixel_slot: int32 [128, 64], P('row', 'col'), may hold values from 0 to 63, as said below
- straddle_dir: int32 [8, 4, 32], P('row', 'col'), may hold values from 0 to 8, as said below
- straddle_slot: int32 [8, 4, 32], P('row', 'col'), may hold values from 0 to 31
- labels: int32 [8, 4, 32], P('row', 'col'), may hold values from 0 to 19
Outputs:
- input_grad: bfloat16 [128, 64, 768], P('row', 'col')
- conv_grad: float32 [3, 3, 64, 128], replicated
- time_grad: float32 [3, 16, 8, 8], replicated
- class_grad: float32 [128, 20], replicated
Inputs may be any that keep to these rules, and one draw needn't show every extreme that they name: `pixel_slot`: below 32 a pixel is in the tile's own parcel of that number, from 32 on in its straddling entry of that number minus 32. Every index of a tile's list is held by at least one pixel of that tile. The owner of entry e of tile (r, c) is tile (r + q // 3 - 1, c + q % 3 - 1) with q = straddle_dir[r, c, e]; q is never 4 and the owner lies within the scene.
All inputs are finite; a program needn't handle non-finite values.
Results may differ from a plain program's by a relative error of at most 0.012.
Values may be sent and summed in bfloat16 or wider, within the bound.
A program may use at most 64 MiB of HBM per device.

v0:
```python
import jax
import jax.numpy as jnp
from jax import lax
from jax.sharding import PartitionSpec as P

DATES = 12
C_IN = 64
C_OUT = 128
GROUPS = 16
CLASSES = 20
P_OWN = 32
S_STR = 32
CPG = 8


EPSILON = 1e-05
PRECISE = lax.Precision.HIGHEST


def with_halo(cells, sides, width):
    for axis, dim in sides:
        count = lax.axis_size(axis)
        ends = count - 1
        head = lax.slice_in_dim(cells, 0, width, axis=dim)
        tail = lax.slice_in_dim(cells, cells.shape[dim] - width, cells.shape[dim], axis=dim)
        cells = jnp.concatenate(
            [
                lax.ppermute(tail, axis, [(i, (i + 1) % count) for i in range(ends)]),
                cells,
                lax.ppermute(head, axis, [((i + 1) % count, i) for i in range(ends)]),
            ],
            axis=dim,
        )
    return cells


def silu_slope(value):
    sig = jax.nn.sigmoid(value)
    return sig * (1.0 + value * (1.0 - sig))


def spatial_forward(padded, conv_weight, tile_rows, tile_cols):
    running_sum = None
    for row_tap in range(3):
        tap_patch = jnp.concatenate(
            [
                padded[row_tap : row_tap + tile_rows, col_tap : col_tap + tile_cols]
                for col_tap in range(3)
            ],
            axis=-1,
        )
        tap_term = jnp.dot(
            tap_patch,
            conv_weight[row_tap].reshape(3 * C_IN, C_OUT),
            preferred_element_type=jnp.float32,
        )
        running_sum = tap_term if running_sum is None else running_sum + tap_term
    return running_sum


def transposed_conv(padded_grad, conv_weight, out_rows, out_cols):
    input_sum = None
    for row_tap in range(3):
        grad_patch = jnp.concatenate(
            [
                padded_grad[
                    2 - row_tap : 2 - row_tap + out_rows, 2 - col_tap : 2 - col_tap + out_cols
                ]
                for col_tap in range(3)
            ],
            axis=-1,
        )
        flipped = jnp.concatenate([conv_weight[row_tap, col_tap].T for col_tap in range(3)], axis=0)
        tap_term = jnp.dot(grad_patch, flipped, preferred_element_type=jnp.float32)
        input_sum = tap_term if input_sum is None else input_sum + tap_term
    return input_sum


def block_weights(time_weight):
    group_eye = jnp.eye(GROUPS, dtype=jnp.bfloat16)
    return jnp.einsum("kgco,gh->kgcho", time_weight, group_eye).reshape(3, C_OUT, C_OUT)


def per_device(
    pixels, conv_weight, time_weight, class_weight, pixel_slot, straddle_dir, straddle_slot, labels
):
    tile_rows, tile_cols = (pixels.shape[0], pixels.shape[1])
    slot_count = P_OWN + S_STR
    padded_pixels = with_halo(pixels, (("row", 0), ("col", 1)), 1).reshape(
        tile_rows + 2, tile_cols + 2, DATES, C_IN
    )
    pre_act = spatial_forward(padded_pixels, conv_weight, tile_rows, tile_cols)
    hidden = jax.nn.silu(pre_act).astype(jnp.bfloat16)
    dense_time = block_weights(time_weight)
    padded_hidden = jnp.pad(hidden, ((0, 0), (0, 0), (1, 1), (0, 0)))
    mixed_time = None
    for time_tap in range(3):
        tap_term = jnp.dot(
            padded_hidden[:, :, time_tap : time_tap + DATES],
            dense_time[time_tap],
            preferred_element_type=jnp.float32,
        )
        mixed_time = tap_term if mixed_time is None else mixed_time + tap_term
    embedded = (
        jnp.mean(jax.nn.silu(mixed_time), axis=2)
        .astype(jnp.bfloat16)
        .reshape(tile_rows * tile_cols, C_OUT)
    )
    flat_slot = pixel_slot.reshape(tile_rows * tile_cols)
    membership = (jnp.arange(slot_count, dtype=jnp.int32)[:, None] == flat_slot[None, :]).astype(
        jnp.bfloat16
    )
    partial_value = jnp.dot(membership, embedded, preferred_element_type=jnp.float32)
    direction = straddle_dir.reshape(S_STR)
    owner_slot = straddle_slot.reshape(S_STR)
    own_slots = jnp.arange(P_OWN, dtype=jnp.int32)
    target = jnp.concatenate([4 * P_OWN + own_slots, direction * P_OWN + owner_slot])
    select = (jnp.arange(9 * P_OWN, dtype=jnp.int32)[:, None] == target[None, :]).astype(
        jnp.float32
    )
    outgoing = jnp.dot(select, partial_value, precision=PRECISE).reshape(3, 3, P_OWN, C_OUT)
    border = with_halo(outgoing.astype(jnp.bfloat16), (("row", 0), ("col", 1)), 1).astype(
        outgoing.dtype
    )
    parcel_sums = jnp.sum(border[0::2, 0::2], axis=(0, 1))
    centered = parcel_sums - jnp.mean(parcel_sums, axis=-1, keepdims=True)
    variance = jnp.mean(centered * centered, axis=-1, keepdims=True)
    inverse = lax.rsqrt(variance + EPSILON)
    normed = centered * inverse
    rounded = normed.astype(jnp.bfloat16)
    logits = jnp.dot(rounded, class_weight, preferred_element_type=jnp.float32)
    exp_logits = jnp.exp(logits)
    probability = exp_logits / jnp.sum(exp_logits, axis=-1, keepdims=True)
    label_hot = (
        labels.reshape(P_OWN)[:, None] == jnp.arange(CLASSES, dtype=jnp.int32)[None, :]
    ).astype(jnp.float32)
    parcel_total = P_OWN * lax.axis_size("row") * lax.axis_size("col")
    grad_logits = (probability - label_hot) / parcel_total
    class_term = jnp.dot(rounded.astype(jnp.float32).T, grad_logits, precision=PRECISE)
    class_grad = lax.psum(class_term, ("row", "col"))
    grad_normed = jnp.dot(grad_logits, class_weight.astype(jnp.float32).T, precision=PRECISE)
    parcel_grad = (
        inverse
        * (
            grad_normed
            - jnp.mean(grad_normed, axis=-1, keepdims=True)
            - normed * jnp.mean(grad_normed * normed, axis=-1, keepdims=True)
        )
    ).astype(jnp.bfloat16)
    beside_all = with_halo(
        parcel_grad.reshape(1, 1, P_OWN, C_OUT), (("row", 0), ("col", 1)), 1
    ).reshape(9 * P_OWN, C_OUT)
    picker = (target[:, None] == jnp.arange(9 * P_OWN, dtype=jnp.int32)[None, :]).astype(
        jnp.bfloat16
    )
    slot_grad = jnp.dot(picker, beside_all, preferred_element_type=jnp.float32).astype(jnp.bfloat16)
    pixel_grad = jnp.dot(membership.T, slot_grad, preferred_element_type=jnp.float32).reshape(
        tile_rows, tile_cols, C_OUT
    )
    grad_mixed = ((pixel_grad / DATES)[:, :, None, :] * silu_slope(mixed_time)).astype(jnp.bfloat16)
    group_eye = jnp.eye(GROUPS, dtype=jnp.float32)
    time_taps = []
    for time_tap in range(3):
        dense_grad = jnp.einsum(
            "ijtc,ijtd->cd",
            padded_hidden[:, :, time_tap : time_tap + DATES],
            grad_mixed,
            preferred_element_type=jnp.float32,
        )
        reshaped = dense_grad.reshape(GROUPS, CPG, GROUPS, CPG)
        time_taps.append(jnp.einsum("gchd,gh->gcd", reshaped, group_eye, precision=PRECISE))
    time_term = jnp.stack(time_taps)
    time_grad = lax.psum(time_term, ("row", "col"))
    padded_mixed = jnp.pad(grad_mixed, ((0, 0), (0, 0), (1, 1), (0, 0)))
    grad_hidden = None
    for time_tap in range(3):
        tap_term = jnp.dot(
            padded_mixed[:, :, 2 - time_tap : 2 - time_tap + DATES],
            dense_time[time_tap].T,
            preferred_element_type=jnp.float32,
        )
        grad_hidden = tap_term if grad_hidden is None else grad_hidden + tap_term
    grad_pre = (grad_hidden * silu_slope(pre_act)).astype(jnp.bfloat16)
    conv_rows = []
    for row_tap in range(3):
        tap_patch = jnp.concatenate(
            [
                padded_pixels[row_tap : row_tap + tile_rows, col_tap : col_tap + tile_cols]
                for col_tap in range(3)
            ],
            axis=-1,
        )
        conv_rows.append(
            jnp.einsum(
                "ijtc,ijtd->cd", tap_patch, grad_pre, preferred_element_type=jnp.float32
            ).reshape(3, C_IN, C_OUT)
        )
    conv_term = jnp.stack(conv_rows)
    padded_grad = with_halo(
        grad_pre.reshape(tile_rows, tile_cols, DATES * C_OUT), (("row", 0), ("col", 1)), 1
    ).reshape(tile_rows + 2, tile_cols + 2, DATES, C_OUT)
    input_sum = transposed_conv(padded_grad, conv_weight, tile_rows, tile_cols)
    input_grad = input_sum.astype(jnp.bfloat16).reshape(tile_rows, tile_cols, DATES * C_IN)
    conv_grad = lax.psum(conv_term, ("row", "col"))
    return (input_grad, conv_grad, time_grad, class_grad)


def solution(mesh):
    in_specs = (
        P("row", "col", None),
        P(),
        P(),
        P(),
        P("row", "col"),
        P("row", "col", None),
        P("row", "col", None),
        P("row", "col", None),
    )
    out_specs = (P("row", "col", None), P(), P(), P())
    return jax.shard_map(
        per_device, mesh=mesh, in_specs=in_specs, out_specs=out_specs, check_vma=False
    )
```

profile of v0, /device:TPU:0, one launch (start us, length us, event | category | flops | bytes accessed | tf_op | source)
XLA Modules:
  0.0 224.2 jit_solution(11208248449679856793)
XLA Ops:
  8.0 4.8 %collective-permute-start = (bf16[1,16,768]{2,1,0:T(8,128)(2,1)S(1)}, bf16[1,16,768]{2,1,0:T(8,128)(2,1)S(1)}, u32[]{:S(2)}, u32[]{:S(2)}) collective-permute-start(bf16[1,16,768]{2,1,0:T(8,128)(2,1)S(1)} %get-tuple-element.38), channel_id=1, source_target_pairs={{0,4},{4,8},{8,12},{12,16},{16,20},{20,24},{24,28},{1,5},{5,9},{9,... | collective-permute-start | bytes 73736 | tf_op jit(solution)/shard_map/ppermute | solution.py:28
  12.8 1.3 collective-permute-start.1
  17.2 1.3 collective-permute-done.1
  18.6 1.3 collective-permute-start.2
  22.9 1.9 collective-permute-done.3
  26.0 2.6 %fusion.81 = (bf16[16,16,12,64]{3,2,1,0:T(8,128)(2,1)S(1)}, bf16[16,16,12,64]{3,2,1,0:T(8,128)(2,1)S(1)}, bf16[16,16,12,64]{3,2,1,0:T(8,128)(2,1)S(1)}, bf16[16,...) fusion(bf16[18,18,12,64]{3,2,1,0:T(8,128)(2,1)S(1)} %reshape.91), kind=kLoop, calls=%fused_computation.148 | loop fusion | bytes 7077888 | tf_op jit(solution)/shard_map/slice | solution.py:47
  32.4 2.4 %multiply_convert_fusion.2 = (bf16[16,16,12,128]{3,1,2,0:T(8,128)(2,1)S(1)}, f32[16,16,12,128]{3,1,2,0:T(8,128)}) fusion(bf16[192,128,1,1]{1,0,3,2:T(8,128)(2,1)S(1)} %bitcast.190, bf16[16,16,12,64]{3,1,2,0:T(8,128)(2,1)S(1)} %copy.63, bf16[16,16,12,64]{3,1,2,0:T(8,128)(2,1)S(1)} %copy.62, bf16[16,16,12,64]{3,1,2,0:T(8,128)(2,1)S(1)} %copy.61, ...), kind=kOutput, calls=%fused_computation.28 | convolution fusion | flops 157286400 | bytes 6733824 | tf_op jit(solution)/shard_map/dot_general | solution.py:52
  36.6 4.4 %collective-permute-start.4 = (bf16[1,3,32,128]{3,2,1,0:T(8,128)(2,1)S(1)}, bf16[1,3,32,128]{3,2,1,0:T(8,128)(2,1)S(1)}, u32[]{:S(2)}, u32[]{:S(2)}) collective-permute-start(bf16[1,3,32,128]{3,2,1,0:T(8,128)(2,1)S(1)} %bitcast.197), channel_id=1, source_target_pairs={{0,4},{4,8},{8,12},{12,16},{16,20},{20,24},{24,28},{1,5},{5,9},{9,... | collective-permute-start | bytes 73736 | tf_op jit(solution)/shard_map/ppermute | solution.py:28
  42.5 4.2 %collective-permute-done.5 = bf16[1,3,32,128]{3,2,1,0:T(8,128)(2,1)S(1)} collective-permute-done((bf16[1,3,32,128]{3,2,1,0:T(8,128)(2,1)S(1)}, bf16[1,3,32,128]{3,2,1,0:T(8,128)(2,1)S(1)}, u32[]{:S(2)}, u32[]{:S(2)}) %collective-permute-start.5) | collective-permute-done | bytes 24608 | tf_op jit(solution)/shard_map/ppermute | solution.py:30
  46.7 3.3 %collective-permute-start.6 = (bf16[5,1,32,128]{3,2,1,0:T(8,128)(2,1)S(1)}, bf16[5,1,32,128]{3,2,1,0:T(8,128)(2,1)S(1)}, u32[]{:S(2)}, u32[]{:S(2)}) collective-permute-start(bf16[5,1,32,128]{3,2,1,0:T(8,128)(2,1)S(1)} %get-tuple-element.51), channel_id=1, source_target_pairs={{0,1},{1,2},{2,3},{4,5},{5,6},{6,7},{8,9},{9,10},{10,11},{12,13},{... | collective-permute-start | bytes 122888 | tf_op jit(solution)/shard_map/ppermute | solution.py:28
  51.9 2.1 collective-permute-done.7
  55.1 4.1 %collective-permute-start.8 = (bf16[1,1,32,128]{3,2,1,0:T(8,128)(2,1)S(1)}, bf16[1,1,32,128]{3,2,1,0:T(8,128)(2,1)S(1)}, u32[]{:S(2)}, u32[]{:S(2)}) collective-permute-start(bf16[1,1,32,128]{3,2,1,0:T(8,128)(2,1)S(1)} %fusion.60), channel_id=1, source_target_pairs={{0,4},{4,8},{8,12},{12,16},{16,20},{20,24},{24,28},{1,5},{5,9},{9,... | collective-permute-start | bytes 24584 | tf_op jit(solution)/shard_map/ppermute | solution.py:28
  60.5 4.2 %collective-permute-done.9 = bf16[1,1,32,128]{3,2,1,0:T(8,128)(2,1)S(1)} collective-permute-done((bf16[1,1,32,128]{3,2,1,0:T(8,128)(2,1)S(1)}, bf16[1,1,32,128]{3,2,1,0:T(8,128)(2,1)S(1)}, u32[]{:S(2)}, u32[]{:S(2)}) %collective-permute-start.9) | collective-permute-done | bytes 8224 | tf_op jit(solution)/shard_map/ppermute | solution.py:30
  64.7 3.2 %collective-permute-start.10 = (bf16[3,1,32,128]{3,2,1,0:T(8,128)(2,1)S(1)}, bf16[3,1,32,128]{3,2,1,0:T(8,128)(2,1)S(1)}, u32[]{:S(2)}, u32[]{:S(2)}) collective-permute-start(bf16[3,1,32,128]{3,2,1,0:T(8,128)(2,1)S(1)} %pad_maximum_fusion.18), channel_id=1, source_target_pairs={{0,1},{1,2},{2,3},{4,5},{5,6},{6,7},{8,9},{9,10},{10,11},{12,13},{... | collective-permute-start | bytes 73736 | tf_op jit(solution)/shard_map/ppermute | solution.py:28
  67.9 1.5 collective-permute-start.11
  69.6 2.3 %collective-permute-done.11 = bf16[3,1,32,128]{3,2,1,0:T(8,128)(2,1)S(1)} collective-permute-done((bf16[3,1,32,128]{3,2,1,0:T(8,128)(2,1)S(1)}, bf16[3,1,32,128]{3,2,1,0:T(8,128)(2,1)S(1)}, u32[]{:S(2)}, u32[]{:S(2)}) %collective-permute-start.11) | collective-permute-done | bytes 24608 | tf_op jit(solution)/shard_map/ppermute | solution.py:30
  85.2 3.6 %collective-permute-start.12 = (bf16[1,16,1536]{2,1,0:T(8,128)(2,1)S(1)}, bf16[1,16,1536]{2,1,0:T(8,128)(2,1)S(1)}, u32[]{:S(2)}, u32[]{:S(2)}) collective-permute-start(bf16[1,16,1536]{2,1,0:T(8,128)(2,1)S(1)} %bitcast.193), channel_id=1, source_target_pairs={{0,4},{4,8},{8,12},{12,16},{16,20},{20,24},{24,28},{1,5},{5,9},{9,... | collective-permute-start | bytes 147464 | tf_op jit(solution)/shard_map/ppermute | solution.py:28
  91.2 4.6 %collective-permute-done.13 = bf16[1,16,1536]{2,1,0:T(8,128)(2,1)S(1)} collective-permute-done((bf16[1,16,1536]{2,1,0:T(8,128)(2,1)S(1)}, bf16[1,16,1536]{2,1,0:T(8,128)(2,1)S(1)}, u32[]{:S(2)}, u32[]{:S(2)}) %collective-permute-start.13) | collective-permute-done | bytes 49184 | tf_op jit(solution)/shard_map/ppermute | solution.py:30
  96.0 3.0 %collective-permute-start.14 = (bf16[18,1,1536]{2,1,0:T(2,128)(2,1)S(1)}, bf16[18,1,1536]{2,1,0:T(2,128)(2,1)S(1)}, u32[]{:S(2)}, u32[]{:S(2)}) collective-permute-start(bf16[18,1,1536]{2,1,0:T(2,128)(2,1)S(1)} %get-tuple-element.31), channel_id=1, source_target_pairs={{0,1},{1,2},{2,3},{4,5},{5,6},{6,7},{8,9},{9,10},{10,11},{12,13},{... | collective-permute-start | bytes 165896 | tf_op jit(solution)/shard_map/ppermute | solution.py:28
  100.4 45.1 %all-reduce.2 = (f32[3,16,8,8]{1,3,2,0:T(8,128)}, f32[128,20]{0,1:T(8,128)}) all-reduce(f32[3,16,8,8]{1,3,2,0:T(8,128)S(1)} %pad_maximum_fusion.13, f32[128,20]{0,1:T(8,128)S(1)} %fusion.63), channel_id=1, replica_groups=mesh['row'=8,'col'=4] {'row','col'}, use_global_device_ids=true, to_apply=%region_8.9 | all-reduce | flops 5632 | bytes 45056 | tf_op jit(solution)/shard_map/psum | solution.py:173
  146.9 2.8 %fusion.80 = (bf16[16,16,12,128]{3,2,1,0:T(8,128)(2,1)S(1)}, bf16[16,16,12,128]{3,2,1,0:T(8,128)(2,1)S(1)}, bf16[16,16,12,128]{3,2,1,0:T(8,128)(2,1)S(1)}, bf16[...) fusion(bf16[18,18,12,128]{3,2,1,0:T(8,128)(2,1)S(1)} %reshape.95), kind=kLoop, calls=%fused_computation.147 | loop fusion | bytes 14155776 | tf_op jit(solution)/shard_map/slice | solution.py:66
  154.6 1.4 reshape.96
  156.0 59.6 %all-reduce.5.cloned.1.call-done = f32[3,3,64,128]{3,2,1,0:T(8,128)} async-done(((f32[3,3,64,128]{3,2,1,0:T(8,128)}), f32[3,3,64,128]{3,2,1,0:T(8,128)}) %all-reduce.5.cloned.1.call-update) | async-done | bytes 294928 | tf_op jit(solution)/shard_map/psum | solution.py:204
  215.6 1.7 copy.92
  (177 shorter events, 42.4 us)
Async XLA Ops:
  7.2 47.2 %copy-start = (bf16[128,20]{0,1:T(8,128)(2,1)S(1)}, bf16[128,20]{0,1:T(8,128)(2,1)}, u32[]{:S(2)}) copy-start(bf16[128,20]{0,1:T(8,128)(2,1)} %param.11) | copy-start | bytes 15364
  7.2 208.4 %all-reduce.5.cloned.1.call-start = ((), (), s32[]{:S(2)}) async-start(), calls=%async_computation | async-start | bytes 589824 | tf_op jit(solution)/shard_map/psum | solution.py:204
  8.0 8.9 %collective-permute-start = (bf16[1,16,768]{2,1,0:T(8,128)(2,1)S(1)}, bf16[1,16,768]{2,1,0:T(8,128)(2,1)S(1)}, u32[]{:S(2)}, u32[]{:S(2)}) collective-permute-start(bf16[1,16,768]{2,1,0:T(8,128)(2,1)S(1)} %get-tuple-element.38), channel_id=1, source_target_pairs={{0,4},{4,8},{8,12},{12,16},{16,20},{20,24},{24,28},{1,5},{5,9},{9,... | collective-permute-start | bytes 73736 | tf_op jit(solution)/shard_map/ppermute | solution.py:28
  12.8 5.7 %collective-permute-start.1 = (bf16[1,16,768]{2,1,0:T(8,128)(2,1)S(1)}, bf16[1,16,768]{2,1,0:T(8,128)(2,1)S(1)}, u32[]{:S(2)}, u32[]{:S(2)}) collective-permute-start(bf16[1,16,768]{2,1,0:T(8,128)(2,1)S(1)} %get-tuple-element.37), channel_id=1, source_target_pairs={{4,0},{8,4},{12,8},{16,12},{20,16},{24,20},{28,24},{5,1},{9,5},{13... | collective-permute-start | bytes 73736 | tf_op jit(solution)/shard_map/ppermute | solution.py:30
  16.8 6.0 %copy-start.27 = (s32[16,16]{1,0:T(8,128)S(1)}, s32[16,16]{1,0:T(8,128)}, u32[]{:S(2)}) copy-start(s32[16,16]{1,0:T(8,128)} %param.12) | copy-start | bytes 3076
  18.6 4.3 %collective-permute-start.2 = (bf16[18,1,768]{2,1,0:T(2,128)(2,1)S(1)}, bf16[18,1,768]{2,1,0:T(2,128)(2,1)S(1)}, u32[]{:S(2)}, u32[]{:S(2)}) collective-permute-start(bf16[18,1,768]{2,1,0:T(2,128)(2,1)S(1)} %get-tuple-element.35), channel_id=1, source_target_pairs={{0,1},{1,2},{2,3},{4,5},{5,6},{6,7},{8,9},{9,10},{10,11},{12,13},{... | collective-permute-start | bytes 82952 | tf_op jit(solution)/shard_map/ppermute | solution.py:28
  19.9 4.9 %collective-permute-start.3 = (bf16[18,1,768]{2,1,0:T(2,128)(2,1)S(1)}, bf16[18,1,768]{2,1,0:T(2,128)(2,1)S(1)}, u32[]{:S(2)}, u32[]{:S(2)}) collective-permute-start(bf16[18,1,768]{2,1,0:T(2,128)(2,1)S(1)} %get-tuple-element.36), channel_id=1, source_target_pairs={{1,0},{2,1},{3,2},{5,4},{6,5},{7,6},{9,8},{10,9},{11,10},{13,12},{... | collective-permute-start | bytes 82952 | tf_op jit(solution)/shard_map/ppermute | solution.py:30
  30.2 2.2 %copy-start.8 = (bf16[16,16,12,64]{3,1,2,0:T(8,128)(2,1)}, bf16[16,16,12,64]{3,1,2,0:T(8,128)(2,1)S(1)}, u32[]{:S(2)}) copy-start(bf16[16,16,12,64]{3,1,2,0:T(8,128)(2,1)S(1)} %copy.61) | copy-start | bytes 1179652
  30.4 2.0 copy-start.10
  35.5 15.8 %copy-start.20 = (bf16[3,3,64,128]{3,2,1,0:T(8,128)(2,1)S(1)}, bf16[3,3,64,128]{3,2,1,0:T(8,128)(2,1)}, u32[]{:S(2)}) copy-start(bf16[3,3,64,128]{3,2,1,0:T(8,128)(2,1)} %param.9) | copy-start | bytes 442372
  36.2 18.5 %copy-start.30 = (s32[1,1,32]{2,1,0:T(1,128)S(1)}, s32[1,1,32]{2,1,0:T(1,128)}, u32[]{:S(2)}) copy-start(s32[1,1,32]{2,1,0:T(1,128)} %param.15) | copy-start | bytes 388
  36.6 5.9 %collective-permute-start.4 = (bf16[1,3,32,128]{3,2,1,0:T(8,128)(2,1)S(1)}, bf16[1,3,32,128]{3,2,1,0:T(8,128)(2,1)S(1)}, u32[]{:S(2)}, u32[]{:S(2)}) collective-permute-start(bf16[1,3,32,128]{3,2,1,0:T(8,128)(2,1)S(1)} %bitcast.197), channel_id=1, source_target_pairs={{0,4},{4,8},{8,12},{12,16},{16,20},{20,24},{24,28},{1,5},{5,9},{9,... | collective-permute-start | bytes 73736 | tf_op jit(solution)/shard_map/ppermute | solution.py:28
  41.0 5.7 %collective-permute-start.5 = (bf16[1,3,32,128]{3,2,1,0:T(8,128)(2,1)S(1)}, bf16[1,3,32,128]{3,2,1,0:T(8,128)(2,1)S(1)}, u32[]{:S(2)}, u32[]{:S(2)}) collective-permute-start(bf16[1,3,32,128]{3,2,1,0:T(8,128)(2,1)S(1)} %bitcast.196), channel_id=1, source_target_pairs={{4,0},{8,4},{12,8},{16,12},{20,16},{24,20},{28,24},{5,1},{9,5},{13... | collective-permute-start | bytes 73736 | tf_op jit(solution)/shard_map/ppermute | solution.py:30
  46.7 5.3 %collective-permute-start.6 = (bf16[5,1,32,128]{3,2,1,0:T(8,128)(2,1)S(1)}, bf16[5,1,32,128]{3,2,1,0:T(8,128)(2,1)S(1)}, u32[]{:S(2)}, u32[]{:S(2)}) collective-permute-start(bf16[5,1,32,128]{3,2,1,0:T(8,128)(2,1)S(1)} %get-tuple-element.51), channel_id=1, source_target_pairs={{0,1},{1,2},{2,3},{4,5},{5,6},{6,7},{8,9},{9,10},{10,11},{12,13},{... | collective-permute-start | bytes 122888 | tf_op jit(solution)/shard_map/ppermute | solution.py:28
  50.0 4.0 %collective-permute-start.7 = (bf16[5,1,32,128]{3,2,1,0:T(8,128)(2,1)S(1)}, bf16[5,1,32,128]{3,2,1,0:T(8,128)(2,1)S(1)}, u32[]{:S(2)}, u32[]{:S(2)}) collective-permute-start(bf16[5,1,32,128]{3,2,1,0:T(8,128)(2,1)S(1)} %get-tuple-element.52), channel_id=1, source_target_pairs={{1,0},{2,1},{3,2},{5,4},{6,5},{7,6},{9,8},{10,9},{11,10},{13,12},{... | collective-permute-start | bytes 122888 | tf_op jit(solution)/shard_map/ppermute | solution.py:30
  55.1 5.5 %collective-permute-start.8 = (bf16[1,1,32,128]{3,2,1,0:T(8,128)(2,1)S(1)}, bf16[1,1,32,128]{3,2,1,0:T(8,128)(2,1)S(1)}, u32[]{:S(2)}, u32[]{:S(2)}) collective-permute-start(bf16[1,1,32,128]{3,2,1,0:T(8,128)(2,1)S(1)} %fusion.60), channel_id=1, source_target_pairs={{0,4},{4,8},{8,12},{12,16},{16,20},{20,24},{24,28},{1,5},{5,9},{9,... | collective-permute-start | bytes 24584 | tf_op jit(solution)/shard_map/ppermute | solution.py:28
  59.2 5.5 %collective-permute-start.9 = (bf16[1,1,32,128]{3,2,1,0:T(8,128)(2,1)S(1)}, bf16[1,1,32,128]{3,2,1,0:T(8,128)(2,1)S(1)}, u32[]{:S(2)}, u32[]{:S(2)}) collective-permute-start(bf16[1,1,32,128]{3,2,1,0:T(8,128)(2,1)S(1)} %fusion.60), channel_id=1, source_target_pairs={{4,0},{8,4},{12,8},{16,12},{20,16},{24,20},{28,24},{5,1},{9,5},{13... | collective-permute-start | bytes 24584 | tf_op jit(solution)/shard_map/ppermute | solution.py:30
  64.7 4.9 %collective-permute-start.10 = (bf16[3,1,32,128]{3,2,1,0:T(8,128)(2,1)S(1)}, bf16[3,1,32,128]{3,2,1,0:T(8,128)(2,1)S(1)}, u32[]{:S(2)}, u32[]{:S(2)}) collective-permute-start(bf16[3,1,32,128]{3,2,1,0:T(8,128)(2,1)S(1)} %pad_maximum_fusion.18), channel_id=1, source_target_pairs={{0,1},{1,2},{2,3},{4,5},{5,6},{6,7},{8,9},{9,10},{10,11},{12,13},{... | collective-permute-start | bytes 73736 | tf_op jit(solution)/shard_map/ppermute | solution.py:28
  67.9 4.0 %collective-permute-start.11 = (bf16[3,1,32,128]{3,2,1,0:T(8,128)(2,1)S(1)}, bf16[3,1,32,128]{3,2,1,0:T(8,128)(2,1)S(1)}, u32[]{:S(2)}, u32[]{:S(2)}) collective-permute-start(bf16[3,1,32,128]{3,2,1,0:T(8,128)(2,1)S(1)} %pad_maximum_fusion.18), channel_id=1, source_target_pairs={{1,0},{2,1},{3,2},{5,4},{6,5},{7,6},{9,8},{10,9},{11,10},{13,12},{... | collective-permute-start | bytes 73736 | tf_op jit(solution)/shard_map/ppermute | solution.py:30
  85.2 6.0 %collective-permute-start.12 = (bf16[1,16,1536]{2,1,0:T(8,128)(2,1)S(1)}, bf16[1,16,1536]{2,1,0:T(8,128)(2,1)S(1)}, u32[]{:S(2)}, u32[]{:S(2)}) collective-permute-start(bf16[1,16,1536]{2,1,0:T(8,128)(2,1)S(1)} %bitcast.193), channel_id=1, source_target_pairs={{0,4},{4,8},{8,12},{12,16},{16,20},{20,24},{24,28},{1,5},{5,9},{9,... | collective-permute-start | bytes 147464 | tf_op jit(solution)/shard_map/ppermute | solution.py:28
  89.9 6.0 %collective-permute-start.13 = (bf16[1,16,1536]{2,1,0:T(8,128)(2,1)S(1)}, bf16[1,16,1536]{2,1,0:T(8,128)(2,1)S(1)}, u32[]{:S(2)}, u32[]{:S(2)}) collective-permute-start(bf16[1,16,1536]{2,1,0:T(8,128)(2,1)S(1)} %bitcast.194), channel_id=1, source_target_pairs={{4,0},{8,4},{12,8},{16,12},{20,16},{24,20},{28,24},{5,1},{9,5},{13... | collective-permute-start | bytes 147464 | tf_op jit(solution)/shard_map/ppermute | solution.py:30
  96.0 49.5 %collective-permute-start.14 = (bf16[18,1,1536]{2,1,0:T(2,128)(2,1)S(1)}, bf16[18,1,1536]{2,1,0:T(2,128)(2,1)S(1)}, u32[]{:S(2)}, u32[]{:S(2)}) collective-permute-start(bf16[18,1,1536]{2,1,0:T(2,128)(2,1)S(1)} %get-tuple-element.31), channel_id=1, source_target_pairs={{0,1},{1,2},{2,3},{4,5},{5,6},{6,7},{8,9},{9,10},{10,11},{12,13},{... | collective-permute-start | bytes 165896 | tf_op jit(solution)/shard_map/ppermute | solution.py:28
  99.1 46.4 %collective-permute-start.15 = (bf16[18,1,1536]{2,1,0:T(2,128)(2,1)S(1)}, bf16[18,1,1536]{2,1,0:T(2,128)(2,1)S(1)}, u32[]{:S(2)}, u32[]{:S(2)}) collective-permute-start(bf16[18,1,1536]{2,1,0:T(2,128)(2,1)S(1)} %get-tuple-element.32), channel_id=1, source_target_pairs={{1,0},{2,1},{3,2},{5,4},{6,5},{7,6},{9,8},{10,9},{11,10},{13,12},{... | collective-permute-start | bytes 165896 | tf_op jit(solution)/shard_map/ppermute | solution.py:30
  153.6 63.8 %copy-start.1 = (bf16[128,20]{0,1:T(8,128)(2,1)S(1)}, bf16[128,20]{0,1:T(8,128)(2,1)}, u32[]{:S(2)}) copy-start(bf16[128,20]{0,1:T(8,128)(2,1)} %param.11) | copy-start | bytes 15364
  (25 other events, 31.9 us)
Sparse Core Ops, SparseCore 0:
  90.0 125.6 all-reduce.4
where the time goes:
time: 225 us; the launch traced here: 224 us
  waiting for transfers between devices  80.6 us (36%)
  blocking collectives  45.1 us (20%)
  starting transfers between devices  38.3 us (17%)
  local copies, waits for them, and re-layouts  25.2 us (11%)
  matrix products  16.9 us (8%)
  between operations  15 us (7%)
  other arithmetic  3.07 us (1%)
    psum x1, waiting for transfers between devices, per_device(): conv_grad = lax.psum(conv_term, ('row', 'col'))  59.6 us
    psum x1, blocking collectives, per_device(): time_grad = lax.psum(time_term, ('row', 'col'))  45.1 us
    ppermute x8, starting transfers between devices, with_halo(): lax.ppermute(tail, axis, [(i, (i + 1) % count) for i in range(ends)])  27.8 us
    ppermute x8, waiting for transfers between devices, with_halo(): lax.ppermute(head, axis, [((i + 1) % count, i) for i in range(ends)])  20.7 us
    ppermute x8, starting transfers between devices, with_halo(): lax.ppermute(head, axis, [((i + 1) % count, i) for i in range(ends)])  10.5 us
    unnamed x88, local copies, waits for them, and re-layouts  9.22 us
  transfers between devices with their start and end apart: 17, of which 9 were waited for; matrix products, arithmetic and copies ran while one was open for 7% of the time, Pallas kernels for 0%

commit v1 on v0

v1 whole, which is shorter than its diff:
```python
import functools

import jax
import jax.numpy as jnp
from jax import lax
from jax.experimental import pallas as pl
from jax.experimental.pallas import tpu as pltpu
from jax.sharding import PartitionSpec as P

DATES = 12
C_IN = 64
C_OUT = 128
GROUPS = 16
CLASSES = 20
P_OWN = 32
S_STR = 32
CPG = 8
EPSILON = 1e-05
PRECISE = lax.Precision.HIGHEST
MESH = pl.DeviceIdType.MESH
F32 = jnp.float32
BF16 = jnp.bfloat16

T = 16
PIX = T * T
PAIRS = DATES // 2
LX = DATES * C_IN
LG = DATES * C_OUT
SLOTS = 9 * P_OWN
CONV_ROWS = 9 * C_IN
SMALL_ROWS = 48
DIRS = [d for d in range(9) if d != 4]


def iota(shape, dim):
    return lax.broadcasted_iota(jnp.int32, shape, dim)


def dot(a, b, dims=((1,), (0,)), precision=None):
    return lax.dot_general(
        a, b, (dims, ((), ())), preferred_element_type=F32, precision=precision
    )


def sigmoid(v):
    return 0.5 * jnp.tanh(0.5 * v) + 0.5


def kernel(
    n_row,
    n_col,
    shard,
    x_ref,
    cw_ref,
    tw_ref,
    kw_ref,
    slot_ref,
    sdir_ref,
    sslot_ref,
    lab_ref,
    gx_ref,
    gcw_ref,
    gtw_ref,
    gkw_ref,
    xf,
    xs,
    xc,
    wf,
    wb,
    b4f,
    b4b,
    onehot,
    onehot_t,
    hid,
    gmix,
    hid_t,
    slope_pre,
    slope_mix,
    gpre,
    zs,
    zacc,
    col_send,
    col_recv,
    cor_send,
    cor_recv,
    sum_send,
    sum_recv,
    pgrad,
    beside,
    z_send,
    z_recv,
    part,
    rs_recv,
    bx_recv,
    final,
    px_ss,
    px_rs,
    ps_ss,
    ps_rs,
    pg_ss,
    pg_rs,
    gh_ss,
    gh_rs,
    zc_ss,
    zc_rs,
    rs_ss,
    rs_rs,
    bx_ss,
    bx_rs,
    ag_ss,
    ag_rs,
):
    row = lax.axis_index("row")
    col = lax.axis_index("col")
    n_a = 2 * n_col
    n_b = n_row // 2
    base = lax.div(row, 2)
    a_row = lax.rem(row, 2)
    a_me = a_row * n_col + col

    def a_dev(k):
        q = lax.rem(a_me + k, n_a)
        return q, (base * 2 + lax.div(q, n_col), lax.rem(q, n_col))

    def b_dev(k):
        return (lax.rem(base + k, n_b) * 2 + a_row, col)

    def neighbour(d):
        r = row + (d // 3 - 1)
        c = col + (d % 3 - 1)
        there = (r >= 0) & (r < n_row) & (c >= 0) & (c < n_col)
        return there, (r, c)

    xc[1, 0] = jnp.zeros((T, LX), BF16)
    xc[1, T + 1] = jnp.zeros((T, LX), BF16)
    gpre[0] = jnp.zeros((T, LG), BF16)
    gpre[T + 1] = jnp.zeros((T, LG), BF16)
    col_recv[...] = jnp.zeros(col_recv.shape, BF16)
    cor_recv[...] = jnp.zeros(cor_recv.shape, BF16)
    sum_recv[...] = jnp.zeros(sum_recv.shape, BF16)
    beside[...] = jnp.zeros(beside.shape, BF16)
    z_recv[...] = jnp.zeros(z_recv.shape, BF16)

    barrier = pltpu.get_barrier_semaphore()
    expected = n_a - 1 + n_b - 1
    for d in DIRS:
        there, dev = neighbour(d)
        expected = expected + there.astype(jnp.int32)

        @pl.when(there)
        def _():
            pl.semaphore_signal(barrier, inc=1, device_id=dev, device_id_type=MESH)

    for k in range(1, n_a):
        pl.semaphore_signal(barrier, inc=1, device_id=a_dev(k)[1], device_id_type=MESH)
    for k in range(1, n_b):
        pl.semaphore_signal(barrier, inc=1, device_id=b_dev(k), device_id_type=MESH)

    x_own = x_ref[...].astype(F32).reshape(PIX, LX)
    left, right = [], []
    for p in range(PAIRS):
        xf[p] = x_own[:, p * 128 : (p + 1) * 128]
        left.append(xf[p, pl.ds(0, T, stride=T), :])
        right.append(xf[p, pl.ds(T - 1, T, stride=T), :])
        col_send[0, :, p * 128 : (p + 1) * 128] = left[p].astype(BF16)
        col_send[1, :, p * 128 : (p + 1) * 128] = right[p].astype(BF16)
    which = iota((T, 128), 0)
    for corner, source, at in ((0, left, 0), (1, right, 0), (2, left, T - 1), (3, right, T - 1)):
        block = jnp.zeros((T, 128), F32)
        for p in range(PAIRS):
            piece = source[p][at : at + 1, :]
            block = jnp.where(which == p, jnp.broadcast_to(piece, (T, 128)), block)
        cor_send[corner] = block.astype(BF16)

    pl.semaphore_wait(barrier, expected)

    corner_of = {0: 0, 2: 1, 6: 2, 8: 3}

    def pixel_copy(d, dev):
        o = 8 - d
        if d in corner_of:
            src, dst = cor_send.at[corner_of[d]], cor_recv.at[corner_of[o]]
        elif d == 1:
            src, dst = x_ref.at[0], xc.at[1, T + 1]
        elif d == 7:
            src, dst = x_ref.at[T - 1], xc.at[1, 0]
        elif d == 3:
            src, dst = col_send.at[0], col_recv.at[1]
        else:
            src, dst = col_send.at[1], col_recv.at[0]
        return pltpu.make_async_remote_copy(
            src_ref=src,
            dst_ref=dst,
            send_sem=px_ss.at[d],
            recv_sem=px_rs.at[o],
            device_id=dev,
            device_id_type=MESH,
        )

    def sums_copy(d, dev):
        return pltpu.make_async_remote_copy(
            src_ref=sum_send.at[d],
            dst_ref=sum_recv.at[8 - d],
            send_sem=ps_ss.at[d],
            recv_sem=ps_rs.at[8 - d],
            device_id=dev,
            device_id_type=MESH,
        )

    def grad_copy(d, dev):
        return pltpu.make_async_remote_copy(
            src_ref=pgrad,
            dst_ref=beside.at[8 - d],
            send_sem=pg_ss.at[d],
            recv_sem=pg_rs.at[8 - d],
            device_id=dev,
            device_id_type=MESH,
        )

    def row_copy(d, dev):
        k = 0 if d == 1 else 1
        return pltpu.make_async_remote_copy(
            src_ref=gpre.at[1 if d == 1 else T],
            dst_ref=gpre.at[T + 1 if d == 1 else 0],
            send_sem=gh_ss.at[k],
            recv_sem=gh_rs.at[1 - k],
            device_id=dev,
            device_id_type=MESH,
        )

    def col_copy(d, dev):
        k = 0 if d == 3 else 1
        return pltpu.make_async_remote_copy(
            src_ref=z_send.at[k],
            dst_ref=z_recv.at[1 - k],
            send_sem=zc_ss.at[k],
            recv_sem=zc_rs.at[1 - k],
            device_id=dev,
            device_id_type=MESH,
        )

    def start_all(make, dirs):
        for d in dirs:
            there, dev = neighbour(d)

            @pl.when(there)
            def _():
                make(d, dev).start()

    def wait_recv_all(make, dirs):
        for d in dirs:
            there, dev = neighbour(d)

            @pl.when(there)
            def _():
                make(8 - d, dev).wait_recv()

    def wait_send_all(make, dirs):
        for d in dirs:
            there, dev = neighbour(d)

            @pl.when(there)
            def _():
                make(d, dev).wait_send()

    start_all(pixel_copy, DIRS)

    xc[1, 1 : T + 1] = x_ref[...]
    wf[...] = jnp.zeros(wf.shape, BF16)
    for r in range(3):
        for c in range(3):
            t = r * 3 + c
            w = cw_ref[r, c]
            wf[t * 128 : t * 128 + 64, 0:128] = w
            wf[t * 128 + 64 : t * 128 + 128, 128:256] = w
    for r in range(3):
        for slot_at, c in ((0, 0), (1, 2), (2, 1)):
            t = r * 3 + c
            block = wf[t * 128 : (t + 1) * 128, :].astype(F32)
            wb[r * 256 : (r + 1) * 256, slot_at * 128 : (slot_at + 1) * 128] = block.T.astype(BF16)
    same_group = lax.div(iota((128, 128), 0), CPG) == lax.div(iota((128, 128), 1), CPG)
    spread = (iota((CPG, 128), 0) == lax.rem(iota((CPG, 128), 1), CPG)).astype(F32)
    dense, dense_t = [], []
    for tap in range(3):
        compact = tw_ref[tap].astype(F32).reshape(128, CPG)
        d_tap = jnp.where(same_group, dot(compact, spread), 0.0)
        dense.append(d_tap.astype(BF16))
        dense_t.append(d_tap.T.astype(BF16))
    nothing = jnp.zeros((128, 128), BF16)
    for ref, (one, two, three) in ((b4f, dense), (b4b, dense_t[::-1])):
        for i, (lo, hi) in enumerate(((one, nothing), (two, one), (three, two), (nothing, three))):
            ref[i * 128 : (i + 1) * 128, 0:128] = lo
            ref[i * 128 : (i + 1) * 128, 128:256] = hi
    zero_side = jnp.zeros((PIX, 128), BF16)
    hid[:, 0:128] = zero_side
    hid[:, 128 + LG : 256 + LG] = zero_side
    gmix[:, 0:128] = zero_side
    gmix[:, 128 + LG : 256 + LG] = zero_side

    pick_row = (lax.div(iota((PIX, T), 0), T) == iota((PIX, T), 1)).astype(BF16)
    by_row = dot(pick_row, slot_ref[...].astype(F32).astype(BF16))
    at_col = lax.rem(iota((PIX, T), 0), T) == iota((PIX, T), 1)
    slot_of = jnp.sum(jnp.where(at_col, by_row, 0.0), axis=1, keepdims=True).astype(jnp.int32)
    in_own = (slot_of == iota((PIX, P_OWN), 1)).astype(BF16)
    in_str = (slot_of - P_OWN == iota((PIX, S_STR), 1)).astype(BF16)
    target = sdir_ref[0] * P_OWN + sslot_ref[0]
    sel_own = (iota((SLOTS, P_OWN), 0) == iota((SLOTS, P_OWN), 1) + 4 * P_OWN).astype(BF16)
    sel_str = (iota((SLOTS, S_STR), 0) == target).astype(BF16)
    onehot[...] = (
        dot(sel_own, in_own, ((1,), (1,))) + dot(sel_str, in_str, ((1,), (1,)))
    ).astype(BF16)
    onehot_t[...] = (
        dot(in_own, sel_own, ((1,), (1,))) + dot(in_str, sel_str, ((1,), (1,)))
    ).astype(BF16)

    for p in range(PAIRS):
        lanes = x_own[:, p * 128 : (p + 1) * 128]
        xs[0, p, T : T + PIX] = pltpu.roll(lanes, 1, 0)
        xs[1, p, T : T + PIX] = pltpu.roll(lanes, PIX - 1, 0)
    wait_recv_all(pixel_copy, DIRS)
    for halo in (0, T + 1):
        line = xc[1, halo].astype(F32)
        for p in range(PAIRS):
            lanes = line[:, p * 128 : (p + 1) * 128]
            xs[0, p, halo * T : (halo + 1) * T] = pltpu.roll(lanes, 1, 0)
            xs[1, p, halo * T : (halo + 1) * T] = pltpu.roll(lanes, T - 1, 0)
    for side, at in ((0, 0), (1, T - 1)):
        arrived = col_recv[side].astype(F32)
        top = cor_recv[side].astype(F32)
        bottom = cor_recv[2 + side].astype(F32)
        last = (T + 1) * T
        for p in range(PAIRS):
            lanes = slice(p * 128, (p + 1) * 128)
            xs[side, p, pl.ds(T + at, T, stride=T), :] = arrived[:, lanes]
            xs[side, p, at : at + 1, :] = top[p : p + 1, :]
            xs[side, p, last + at : last + at + 1, :] = bottom[p : p + 1, :]
            xc[2 * side, :, :, lanes] = xs[side, p].astype(BF16).reshape(T + 2, T, 128)

    def taps(p):
        return jnp.concatenate(
            [
                xc[c, r : r + T, :, p * 128 : (p + 1) * 128].reshape(PIX, 128)
                for r in range(3)
                for c in range(3)
            ],
            axis=1,
        )

    for p in range(PAIRS):
        pre = dot(taps(p), wf[...])
        sig = sigmoid(pre)
        act = pre * sig
        slope_pre[:, p * 256 : (p + 1) * 256] = sig + act * (1.0 - sig)
        hid[:, 128 + p * 256 : 128 + (p + 1) * 256] = act.astype(BF16)
    total = jnp.zeros((PIX, 256), F32)
    for p in range(PAIRS):
        mixed = dot(hid[:, p * 256 : p * 256 + 512], b4f[...])
        sig = sigmoid(mixed)
        act = mixed * sig
        slope_mix[:, p * 256 : (p + 1) * 256] = (sig + act * (1.0 - sig)) * (1.0 / DATES)
        total = total + act
    embedded = ((total[:, 0:128] + total[:, 128:256]) * (1.0 / DATES)).astype(BF16)
    outgoing = dot(onehot[...], embedded)
    for d in DIRS:
        sum_send[d] = outgoing[d * P_OWN : (d + 1) * P_OWN].astype(BF16)
    start_all(sums_copy, DIRS)
    sums = outgoing[4 * P_OWN : 5 * P_OWN]
    for p in range(PAIRS):
        hid_t[p * 256 : (p + 1) * 256, :] = hid[:, 128 + p * 256 : 128 + (p + 1) * 256].T
    wait_recv_all(sums_copy, DIRS)
    for d in DIRS:
        sums = sums + sum_recv[d].astype(F32)

    centered = sums - jnp.mean(sums, axis=-1, keepdims=True)
    inverse = lax.rsqrt(jnp.mean(centered * centered, axis=-1, keepdims=True) + EPSILON)
    normed = centered * inverse
    rounded = normed.astype(BF16)
    kw = kw_ref[...]
    logits = dot(rounded, kw)
    exps = jnp.exp(logits)
    prob = exps / jnp.sum(exps, axis=-1, keepdims=True)
    lab = lab_ref[0]
    lab_col = jnp.sum(
        jnp.where(iota((P_OWN, P_OWN), 0) == iota((P_OWN, P_OWN), 1), lab.astype(F32), 0.0),
        axis=1,
        keepdims=True,
    ).astype(jnp.int32)
    hot = (lab_col == iota((P_OWN, CLASSES), 1)).astype(F32)
    g_logits = (prob - hot) * (1.0 / (P_OWN * n_row * n_col))
    g_normed = dot(g_logits, kw.astype(F32), ((1,), (1,)), PRECISE)
    g_parcel = inverse * (
        g_normed
        - jnp.mean(g_normed, axis=-1, keepdims=True)
        - normed * jnp.mean(g_normed * normed, axis=-1, keepdims=True)
    )
    g_parcel = g_parcel.astype(BF16)
    pgrad[...] = g_parcel
    start_all(grad_copy, DIRS)
    beside[4] = g_parcel
    class_term = dot(g_logits, rounded.astype(F32), ((0,), (0,)), PRECISE)
    wait_recv_all(grad_copy, DIRS)

    pixel_grad = dot(onehot_t[...], beside[...].reshape(SLOTS, C_OUT))
    pixel_grad = jnp.concatenate([pixel_grad, pixel_grad], axis=1)
    for p in range(PAIRS):
        gmix[:, 128 + p * 256 : 128 + (p + 1) * 256] = (
            pixel_grad * slope_mix[:, p * 256 : (p + 1) * 256]
        ).astype(BF16)
    for p in range(PAIRS):
        g_hid = dot(gmix[:, p * 256 : p * 256 + 512], b4b[...])
        g_pre = (g_hid * slope_pre[:, p * 256 : (p + 1) * 256]).astype(BF16)
        gpre[1 : T + 1, :, p * 256 : (p + 1) * 256] = g_pre.reshape(T, T, 256)
    start_all(row_copy, (1, 7))

    conv_t = None
    for p in range(PAIRS):
        g_pair = gpre[1 : T + 1, :, p * 256 : (p + 1) * 256].reshape(PIX, 256)
        term = dot(g_pair, taps(p), ((0,), (0,)))
        conv_t = term if conv_t is None else conv_t + term
    low_half = iota((128, 128), 1) < C_IN
    for t in range(9):
        both = jnp.where(
            low_half,
            conv_t[0:128, t * 128 : (t + 1) * 128],
            conv_t[128:256, t * 128 : (t + 1) * 128],
        ).T
        part[t * 64 : (t + 1) * 64, :] = (both[0:64] + both[64:128]).astype(BF16)
    even = None
    for p in range(PAIRS):
        term = dot(
            hid_t[p * 256 : (p + 1) * 256, :], gmix[:, 128 + p * 256 : 128 + (p + 1) * 256]
        )
        even = term if even is None else even + term
    odd = None
    for p in range(PAIRS - 1):
        term = dot(
            hid_t[p * 256 + 128 : p * 256 + 384, :],
            gmix[:, 256 + p * 256 : 512 + p * 256],
        )
        odd = term if odd is None else odd + term
    time_taps = (
        even[0:128, 128:256] + odd[0:128, 128:256],
        even[0:128, 0:128] + even[128:256, 128:256],
        even[128:256, 0:128] + odd[128:256, 0:128],
    )
    small = [
        jnp.sum(jnp.where(same_group, tap, 0.0).reshape(GROUPS, CPG, 128), axis=0)
        for tap in time_taps
    ]
    small.append(class_term)
    small.append(jnp.zeros((SMALL_ROWS - 3 * CPG - CLASSES, 128), F32))
    part[CONV_ROWS : CONV_ROWS + SMALL_ROWS, :] = jnp.concatenate(small, axis=0).astype(BF16)

    def shard_at(q):
        return pl.ds(pl.multiple_of(q * shard, 16), shard)

    def rs_copy(k):
        q, dev = a_dev(k)
        return pltpu.make_async_remote_copy(
            src_ref=part.at[shard_at(q)],
            dst_ref=rs_recv.at[k],
            send_sem=rs_ss.at[k],
            recv_sem=rs_rs.at[k],
            device_id=dev,
            device_id_type=MESH,
        )

    def bx_copy(k):
        return pltpu.make_async_remote_copy(
            src_ref=bx_recv.at[base],
            dst_ref=bx_recv.at[base],
            send_sem=bx_ss.at[k],
            recv_sem=bx_rs.at[k],
            device_id=b_dev(k),
            device_id_type=MESH,
        )

    def ag_copy(k):
        return pltpu.make_async_remote_copy(
            src_ref=final.at[shard_at(a_me)],
            dst_ref=final.at[shard_at(a_me)],
            send_sem=ag_ss.at[k],
            recv_sem=ag_rs.at[k],
            device_id=a_dev(k)[1],
            device_id_type=MESH,
        )

    for k in range(1, n_a):
        rs_copy(k).start()

    wait_recv_all(row_copy, (1, 7))
    j_at = lax.rem(iota((PIX, 128), 0), T)
    for p in range(PAIRS):
        g_rows = jnp.concatenate(
            [
                gpre[2 - r : 2 - r + T, :, p * 256 : (p + 1) * 256].reshape(PIX, 256)
                for r in range(3)
            ],
            axis=1,
        )
        z = dot(g_rows, wb[...])
        zs[0] = z[:, 0:128]
        zs[1] = z[:, 128:256]
        z_send[0, :, p * 128 : (p + 1) * 128] = zs[0, pl.ds(0, T, stride=T), :].astype(BF16)
        z_send[1, :, p * 128 : (p + 1) * 128] = zs[1, pl.ds(T - 1, T, stride=T), :].astype(BF16)
        from_right = jnp.where(j_at == T - 1, 0.0, pltpu.roll(z[:, 0:128], PIX - 1, 0))
        from_left = jnp.where(j_at == 0, 0.0, pltpu.roll(z[:, 128:256], 1, 0))
        zacc[p] = z[:, 256:384] + from_right + from_left
    start_all(col_copy, (3, 5))

    mine = part[shard_at(a_me)].astype(F32)
    for k in range(1, n_a):
        rs_copy(k).wait_recv()
    for k in range(1, n_a):
        mine = mine + rs_recv[k].astype(F32)
    bx_recv[base] = mine.astype(BF16)
    for k in range(1, n_b):
        bx_copy(k).start()

    wait_recv_all(col_copy, (3, 5))
    for p in range(PAIRS):
        lanes = slice(p * 128, (p + 1) * 128)
        at_left = zacc[p, pl.ds(0, T, stride=T), :] + z_recv[0, :, lanes].astype(F32)
        zacc[p, pl.ds(0, T, stride=T), :] = at_left
        at_right = zacc[p, pl.ds(T - 1, T, stride=T), :] + z_recv[1, :, lanes].astype(F32)
        zacc[p, pl.ds(T - 1, T, stride=T), :] = at_right
        gx_ref[:, :, lanes] = zacc[p].astype(BF16).reshape(T, T, 128)

    for k in range(1, n_b):
        pltpu.make_async_remote_copy(
            src_ref=bx_recv.at[base],
            dst_ref=bx_recv.at[lax.rem(base + n_b - k, n_b)],
            send_sem=bx_ss.at[k],
            recv_sem=bx_rs.at[k],
            device_id=b_dev(k),
            device_id_type=MESH,
        ).wait_recv()
    whole = bx_recv[0].astype(F32)
    for g in range(1, n_b):
        whole = whole + bx_recv[g].astype(F32)
    final[shard_at(a_me)] = whole.astype(BF16)
    for k in range(1, n_a):
        ag_copy(k).start()
    wait_send_all(pixel_copy, DIRS)
    wait_send_all(sums_copy, DIRS)
    wait_send_all(grad_copy, DIRS)
    wait_send_all(row_copy, (1, 7))
    wait_send_all(col_copy, (3, 5))
    for k in range(1, n_a):
        rs_copy(k).wait_send()
    for k in range(1, n_b):
        bx_copy(k).wait_send()
    for k in range(1, n_a):
        q = lax.rem(a_me + n_a - k, n_a)
        pltpu.make_async_remote_copy(
            src_ref=final.at[shard_at(a_me)],
            dst_ref=final.at[shard_at(q)],
            send_sem=ag_ss.at[k],
            recv_sem=ag_rs.at[k],
            device_id=a_dev(k)[1],
            device_id_type=MESH,
        ).wait_recv()
    for t in range(9):
        gcw_ref[t // 3, t % 3] = final[t * 64 : (t + 1) * 64, :].astype(F32)
    small_sum = final[CONV_ROWS : CONV_ROWS + SMALL_ROWS, :].astype(F32)
    for tap in range(3):
        for g in range(GROUPS):
            gtw_ref[tap, g] = small_sum[tap * CPG : (tap + 1) * CPG, g * CPG : (g + 1) * CPG]
    class_rows = jnp.concatenate(
        [small_sum[3 * CPG : SMALL_ROWS], jnp.zeros((128 - SMALL_ROWS + 3 * CPG, 128), F32)], axis=0
    )
    gkw_ref[...] = class_rows.T[:, 0:CLASSES]
    for k in range(1, n_a):
        ag_copy(k).wait_send()


def per_device(n_row, n_col, *args):
    n_a = 2 * n_col
    n_b = n_row // 2
    rows = CONV_ROWS + SMALL_ROWS
    shard = -(-rows // (16 * n_a)) * 16
    total = shard * n_a
    vmem = pl.BlockSpec(memory_space=pltpu.VMEM)
    dma = pltpu.SemaphoreType.DMA
    return pl.pallas_call(
        functools.partial(kernel, n_row, n_col, shard),
        out_shape=(
            jax.ShapeDtypeStruct((T, T, LX), BF16),
            jax.ShapeDtypeStruct((3, 3, C_IN, C_OUT), F32),
            jax.ShapeDtypeStruct((3, GROUPS, CPG, CPG), F32),
            jax.ShapeDtypeStruct((C_OUT, CLASSES), F32),
        ),
        in_specs=[vmem] * 8,
        out_specs=(vmem,) * 4,
        scratch_shapes=[
            pltpu.VMEM((PAIRS, PIX, 128), F32),
            pltpu.VMEM((2, PAIRS, PIX + 2 * T, 128), F32),
            pltpu.VMEM((3, T + 2, T, LX), BF16),
            pltpu.VMEM((9 * 128, 256), BF16),
            pltpu.VMEM((3 * 256, 3 * 128), BF16),
            pltpu.VMEM((512, 256), BF16),
            pltpu.VMEM((512, 256), BF16),
            pltpu.VMEM((SLOTS, PIX), BF16),
            pltpu.VMEM((PIX, SLOTS), BF16),
            pltpu.VMEM((PIX, LG + 256), BF16),
            pltpu.VMEM((PIX, LG + 256), BF16),
            pltpu.VMEM((LG, PIX), BF16),
            pltpu.VMEM((PIX, LG), F32),
            pltpu.VMEM((PIX, LG), F32),
            pltpu.VMEM((T + 2, T, LG), BF16),
            pltpu.VMEM((2, PIX, 128), F32),
            pltpu.VMEM((PAIRS, PIX, 128), F32),
            pltpu.VMEM((2, T, LX), BF16),
            pltpu.VMEM((2, T, LX), BF16),
            pltpu.VMEM((4, T, 128), BF16),
            pltpu.VMEM((4, T, 128), BF16),
            pltpu.VMEM((9, P_OWN, C_OUT), BF16),
            pltpu.VMEM((9, P_OWN, C_OUT), BF16),
            pltpu.VMEM((P_OWN, C_OUT), BF16),
            pltpu.VMEM((9, P_OWN, C_OUT), BF16),
            pltpu.VMEM((2, T, LX), BF16),
            pltpu.VMEM((2, T, LX), BF16),
            pltpu.VMEM((total, 128), BF16),
            pltpu.VMEM((n_a, shard, 128), BF16),
            pltpu.VMEM((n_b, shard, 128), BF16),
            pltpu.VMEM((total, 128), BF16),
            dma((9,)),
            dma((9,)),
            dma((9,)),
            dma((9,)),
            dma((9,)),
            dma((9,)),
            dma((2,)),
            dma((2,)),
            dma((2,)),
            dma((2,)),
            dma((n_a,)),
            dma((n_a,)),
            dma((n_b,)),
            dma((n_b,)),
            dma((n_a,)),
            dma((n_a,)),
        ],
        compiler_params=pltpu.CompilerParams(
            collective_id=0, has_side_effects=True, vmem_limit_bytes=40 * 1024 * 1024
        ),
    )(*args)


def solution(mesh):
    in_specs = (
        P("row", "col", None),
        P(),
        P(),
        P(),
        P("row", "col"),
        P("row", "col", None),
        P("row", "col", None),
        P("row", "col", None),
    )
    out_specs = (P("row", "col", None), P(), P(), P())
    return jax.shard_map(
        functools.partial(per_device, mesh.shape["row"], mesh.shape["col"]),
        mesh=mesh,
        in_specs=in_specs,
        out_specs=out_specs,
        check_vma=False,
    )
```

time: 225 us -> 40.5 us (0.18)
  waiting for transfers between devices: 80.6 us -> 0 us
  blocking collectives: 45.1 us -> 0 us
  starting transfers between devices: 38.3 us -> 0 us
  Pallas kernels: 0 us -> 33.9 us
  local copies, waits for them, and re-layouts: 25.2 us -> 5.72 us
  matrix products: 16.9 us -> 0 us
  between operations: 15 us -> 0.73 us
  other arithmetic: 3.07 us -> 0 us
    psum x1 -> x0, waiting for transfers between devices: 59.6 us -> none  [per_device(): conv_grad = lax.psum(conv_term, ('row', 'col'))]
    psum x1 -> x0, blocking collectives: 45.1 us -> none  [per_device(): time_grad = lax.psum(time_term, ('row', 'col'))]
    ppermute x16 -> x0, starting transfers between devices: 38.3 us -> none  [the longest x8 27.8 us: with_halo(): lax.ppermute(tail, axis, [(i, (i + 1) % count) for i in range(ends)])]
    pallas_call x0 -> x1, Pallas kernels: none -> 33.9 us  [per_device(): pl.pallas_call(functools.partial(kernel, n_row, n_col, shard), out_shape=...]
    ppermute x16 -> x0, waiting for transfers between devices: 21 us -> none  [the longest x8 20.7 us: with_halo(): lax.ppermute(head, axis, [((i + 1) % count, i) for i in range(ends)])]
    dot_general x27 -> x0, matrix products: 16.9 us -> none  [the longest x3 4.09 us: spatial_forward(): jnp.dot(tap_patch, conv_weight[row_tap].reshape(3 * C_IN, C_OUT), preferr...]
    slice x10 -> x0, local copies, waits for them, and re-layouts: 7.62 us -> none  [the longest x1 2.8 us: transposed_conv(): padded_grad[2 - row_tap:2 - row_tap + out_rows, 2 - col_tap:2 - col_tap +...]
    unnamed x88 -> x16, local copies, waits for them, and re-layouts: 9.22 us -> 4.27 us
  transfers between devices with their start and end apart: 17 -> 0, of which waited for: 9 -> 0; matrix products, arithmetic and copies ran while one was open for 7% -> 0% of each run, Pallas kernels for 0% -> 0%
where the time goes in v1:
time: 40.5 us; the launch traced here: 40.3 us
  Pallas kernels  33.9 us (84%)
  local copies, waits for them, and re-layouts  5.72 us (14%)
  between operations  0.73 us (2%)
    pallas_call x1, Pallas kernels, per_device(): pl.pallas_call(functools.partial(kernel, n_row, n_col, shard), out_shape=...  33.9 us
    unnamed x16, local copies, waits for them, and re-layouts  4.27 us
    pallas_call x2, local copies, waits for them, and re-layouts, per_device(): pl.pallas_call(functools.partial(kernel, n_row, n_col, shard), out_shape=...  1.44 us

profile of v1, /device:TPU:0, one launch (start us, length us, event | category | flops | bytes accessed | tf_op | source)
XLA Modules:
  0.0 40.3 jit_solution(13229393932196523298)
XLA Ops:
  0.6 0.0 copy-start.1
  0.6 0.9 %copy.13.kw_ref = bf16[128,20]{1,0:T(8,128)(2,1)S(1)} copy(bf16[128,20]{0,1:T(8,128)(2,1)} %param.11) | data formatting | bytes 10240 | tf_op args[3]
  1.5 0.0 copy-start.2
  1.5 0.0 copy-start.3
  1.5 0.0 copy-start.4
  1.5 0.0 copy-start.5
  1.5 0.9 %copy.12.tw_ref = bf16[3,16,8,8]{3,2,1,0:T(8,128)(2,1)S(1)} copy(bf16[3,16,8,8]{1,3,2,0:T(8,128)(2,1)} %param.10) | data formatting | bytes 12288 | tf_op args[2]
  2.5 0.0 copy-done.1
  2.5 0.0 copy-done.2
  2.5 0.0 copy-done.3
  2.5 0.0 copy-done.4
  2.5 0.0 copy-done.5
  2.5 0.0 copy-start
  2.5 1.0 %copy-done = bf16[16,16,768]{2,1,0:T(8,128)(2,1)S(1)} copy-done((bf16[16,16,768]{2,1,0:T(8,128)(2,1)S(1)}, bf16[16,16,768]{2,1,0:T(8,128)(2,1)}, u32[]{:S(2)}) %copy-start) | copy-done | bytes 393240
  3.5 33.9 %shard_map.111 = (bf16[16,16,768]{2,1,0:T(8,128)(2,1)S(1)}, f32[3,3,64,128]{3,2,1,0:T(8,128)S(1)}, f32[3,16,8,8]{3,2,1,0:T(8,128)S(1)}, f32[128,20]{1,0:T(8,128)S(1)}) custom-call(bf16[16,16,768]{2,1,0:T(8,128)(2,1)S(1)} %copy-done, bf16[3,3,64,128]{3,2,1,0:T(8,128)(2,1)S(1)} %copy-done.1, bf16[3,16,8,8]{3,2,1,0:T(8,128)(2,1)S(1)} %copy.12.tw_ref, ...), custom_call_target="tpu_custom_call" | custom-call | tf_op jit(solution)/shard_map/pallas_call | solution.py:585
  37.4 0.7 %copy.15 = f32[128,20]{0,1:T(8,128)} copy(f32[128,20]{1,0:T(8,128)S(1)} %get-tuple-element.7) | data formatting | bytes 20480 | tf_op jit(solution)/shard_map/pallas_call | solution.py:585
  38.1 0.8 %copy.14 = f32[3,16,8,8]{1,3,2,0:T(8,128)} copy(f32[3,16,8,8]{3,2,1,0:T(8,128)S(1)} %get-tuple-element.6) | data formatting | bytes 24576 | tf_op jit(solution)/shard_map/pallas_call | solution.py:585
  38.9 0.7 %copy.18 = bf16[16,16,768]{2,1,0:T(8,128)(2,1)} copy(bf16[16,16,768]{2,1,0:T(8,128)(2,1)S(1)} %get-tuple-element.12) | data formatting | bytes 786432
  39.6 0.7 %copy.19 = f32[3,3,64,128]{3,2,1,0:T(8,128)} copy(f32[3,3,64,128]{3,2,1,0:T(8,128)S(1)} %get-tuple-element.13) | data formatting | bytes 589824
Async XLA Ops:
  0.6 1.9 %copy-start.1 = (bf16[3,3,64,128]{3,2,1,0:T(8,128)(2,1)S(1)}, bf16[3,3,64,128]{3,2,1,0:T(8,128)(2,1)}, u32[]{:S(2)}) copy-start(bf16[3,3,64,128]{3,2,1,0:T(8,128)(2,1)} %cw_ref.1) | copy-start | bytes 442372
  1.5 1.0 %copy-start.2 = (s32[16,16]{1,0:T(8,128)S(1)}, s32[16,16]{1,0:T(8,128)}, u32[]{:S(2)}) copy-start(s32[16,16]{1,0:T(8,128)} %slot_ref.1) | copy-start | bytes 3076
  1.5 1.0 %copy-start.3 = (s32[1,1,32]{2,1,0:T(1,128)S(1)}, s32[1,1,32]{2,1,0:T(1,128)}, u32[]{:S(2)}) copy-start(s32[1,1,32]{2,1,0:T(1,128)} %sdir_ref.1) | copy-start | bytes 388
  1.5 1.0 %copy-start.4 = (s32[1,1,32]{2,1,0:T(1,128)S(1)}, s32[1,1,32]{2,1,0:T(1,128)}, u32[]{:S(2)}) copy-start(s32[1,1,32]{2,1,0:T(1,128)} %sslot_ref.1) | copy-start | bytes 388
  1.5 1.0 %copy-start.5 = (s32[1,1,32]{2,1,0:T(1,128)S(1)}, s32[1,1,32]{2,1,0:T(1,128)}, u32[]{:S(2)}) copy-start(s32[1,1,32]{2,1,0:T(1,128)} %lab_ref.1) | copy-start | bytes 388
  2.5 1.0 %copy-start = (bf16[16,16,768]{2,1,0:T(8,128)(2,1)S(1)}, bf16[16,16,768]{2,1,0:T(8,128)(2,1)}, u32[]{:S(2)}) copy-start(bf16[16,16,768]{2,1,0:T(8,128)(2,1)} %x_ref.1) | copy-start | bytes 1179652

commit v2 on v1

--- a/solution.py
+++ b/solution.py
@@ -21,6 +21,7 @@
 F32 = jnp.float32
 BF16 = jnp.bfloat16
 
+VMEM_GRANT = 63 * 1024 * 1024
 T = 16
 PIX = T * T
 PAIRS = DATES // 2
@@ -50,6 +51,19 @@
     n_row,
     n_col,
     shard,
+    x_hbm,
+    cw_hbm,
+    tw_hbm,
+    kw_hbm,
+    slot_hbm,
+    sdir_hbm,
+    sslot_hbm,
+    lab_hbm,
+    gx_hbm,
+    final_hbm,
+    gx_ref,
+    final,
+    out_sems,
     x_ref,
     cw_ref,
     tw_ref,
@@ -58,10 +72,7 @@
     sdir_ref,
     sslot_ref,
     lab_ref,
-    gx_ref,
-    gcw_ref,
-    gtw_ref,
-    gkw_ref,
+    in_sems,
     xf,
     xs,
     xc,
@@ -92,7 +103,6 @@
     part,
     rs_recv,
     bx_recv,
-    final,
     px_ss,
     px_rs,
     ps_ss,
@@ -131,6 +141,24 @@
         there = (r >= 0) & (r < n_row) & (c >= 0) & (c < n_col)
         return there, (r, c)
 
+    fetches = [
+        pltpu.make_async_copy(src, dst, in_sems.at[i])
+        for i, (src, dst) in enumerate(
+            (
+                (x_hbm, x_ref),
+                (cw_hbm, cw_ref),
+                (tw_hbm, tw_ref),
+                (kw_hbm, kw_ref),
+                (slot_hbm, slot_ref),
+                (sdir_hbm, sdir_ref),
+                (sslot_hbm, sslot_ref),
+                (lab_hbm, lab_ref),
+            )
+        )
+    ]
+    for fetch in fetches:
+        fetch.start()
+
     xc[1, 0] = jnp.zeros((T, LX), BF16)
     xc[1, T + 1] = jnp.zeros((T, LX), BF16)
     gpre[0] = jnp.zeros((T, LG), BF16)
@@ -156,6 +184,7 @@
     for k in range(1, n_b):
         pl.semaphore_signal(barrier, inc=1, device_id=b_dev(k), device_id_type=MESH)
 
+    fetches[0].wait()
     x_own = x_ref[...].astype(F32).reshape(PIX, LX)
     left, right = [], []
     for p in range(PAIRS):
@@ -265,6 +294,8 @@
 
     start_all(pixel_copy, DIRS)
 
+    for fetch in fetches[1:]:
+        fetch.wait()
     xc[1, 1 : T + 1] = x_ref[...]
     wf[...] = jnp.zeros(wf.shape, BF16)
     for r in range(3):
@@ -279,11 +310,19 @@
             block = wf[t * 128 : (t + 1) * 128, :].astype(F32)
             wb[r * 256 : (r + 1) * 256, slot_at * 128 : (slot_at + 1) * 128] = block.T.astype(BF16)
     same_group = lax.div(iota((128, 128), 0), CPG) == lax.div(iota((128, 128), 1), CPG)
-    spread = (iota((CPG, 128), 0) == lax.rem(iota((CPG, 128), 1), CPG)).astype(F32)
+    width = 3 * CPG * CPG
+    by_group = (lax.div(iota((128, GROUPS), 0), CPG) == iota((128, GROUPS), 1)).astype(BF16)
+    compact = tw_ref[...].astype(F32).reshape(width, GROUPS).astype(BF16)
+    spread_rows = dot(by_group, compact, ((1,), (1,)))
+    entry = iota((128, width), 1)
+    in_chan = lax.rem(iota((128, width), 0), CPG)
+    fold_out = (
+        lax.rem(iota((width, 128), 0), CPG) == lax.rem(iota((width, 128), 1), CPG)
+    ).astype(BF16)
     dense, dense_t = [], []
     for tap in range(3):
-        compact = tw_ref[tap].astype(F32).reshape(128, CPG)
-        d_tap = jnp.where(same_group, dot(compact, spread), 0.0)
+        rows = jnp.where(lax.div(entry, CPG) == tap * CPG + in_chan, spread_rows, 0.0)
+        d_tap = jnp.where(same_group, dot(rows.astype(BF16), fold_out), 0.0)
         dense.append(d_tap.astype(BF16))
         dense_t.append(d_tap.T.astype(BF16))
     nothing = jnp.zeros((128, 128), BF16)
@@ -376,7 +415,7 @@
     normed = centered * inverse
     rounded = normed.astype(BF16)
     kw = kw_ref[...]
-    logits = dot(rounded, kw)
+    logits = dot(rounded, kw, ((1,), (1,)))
     exps = jnp.exp(logits)
     prob = exps / jnp.sum(exps, axis=-1, keepdims=True)
     lab = lab_ref[0]
@@ -387,7 +426,7 @@
     ).astype(jnp.int32)
     hot = (lab_col == iota((P_OWN, CLASSES), 1)).astype(F32)
     g_logits = (prob - hot) * (1.0 / (P_OWN * n_row * n_col))
-    g_normed = dot(g_logits, kw.astype(F32), ((1,), (1,)), PRECISE)
+    g_normed = dot(g_logits, kw.astype(F32), ((1,), (0,)), PRECISE)
     g_parcel = inverse * (
         g_normed
         - jnp.mean(g_normed, axis=-1, keepdims=True)
@@ -526,6 +565,8 @@
         zacc[p, pl.ds(T - 1, T, stride=T), :] = at_right
         gx_ref[:, :, lanes] = zacc[p].astype(BF16).reshape(T, T, 128)
 
+    gx_store = pltpu.make_async_copy(gx_ref, gx_hbm, out_sems.at[0])
+    gx_store.start()
     for k in range(1, n_b):
         pltpu.make_async_remote_copy(
             src_ref=bx_recv.at[base],
@@ -560,21 +601,35 @@
             device_id=a_dev(k)[1],
             device_id_type=MESH,
         ).wait_recv()
+    final_store = pltpu.make_async_copy(final, final_hbm, out_sems.at[1])
+    final_store.start()
+    for k in range(1, n_a):
+        ag_copy(k).wait_send()
+    gx_store.wait()
+    final_store.wait()
+
+
+def finish(gx_in, final, gx_out, gcw_ref, gtw_ref, gkw_ref, sem):
+    copy = pltpu.make_async_copy(gx_in, gx_out, sem)
+    copy.start()
     for t in range(9):
         gcw_ref[t // 3, t % 3] = final[t * 64 : (t + 1) * 64, :].astype(F32)
-    small_sum = final[CONV_ROWS : CONV_ROWS + SMALL_ROWS, :].astype(F32)
-    for tap in range(3):
-        for g in range(GROUPS):
-            gtw_ref[tap, g] = small_sum[tap * CPG : (tap + 1) * CPG, g * CPG : (g + 1) * CPG]
-    class_rows = jnp.concatenate(
-        [small_sum[3 * CPG : SMALL_ROWS], jnp.zeros((128 - SMALL_ROWS + 3 * CPG, 128), F32)], axis=0
+    width = 3 * CPG * CPG
+    small = final[CONV_ROWS : CONV_ROWS + SMALL_ROWS, :]
+    repeat = (lax.div(iota((width, SMALL_ROWS), 0), CPG) == iota((width, SMALL_ROWS), 1)).astype(
+        BF16
     )
-    gkw_ref[...] = class_rows.T[:, 0:CLASSES]
-    for k in range(1, n_a):
-        ag_copy(k).wait_send()
-
-
-def per_device(n_row, n_col, *args):
+    rows = dot(repeat, small)
+    own_out = lax.rem(iota((width, 128), 0), CPG) == lax.rem(iota((width, 128), 1), CPG)
+    fold = (lax.div(iota((128, GROUPS), 0), CPG) == iota((128, GROUPS), 1)).astype(BF16)
+    rows = jnp.where(own_out, rows, 0.0).astype(BF16)
+    gtw_ref[...] = dot(rows, fold).reshape(3, CPG, CPG, GROUPS)
+    gkw_ref[...] = small[3 * CPG : 3 * CPG + CLASSES].astype(F32)
+    copy.wait()
+
+
+def per_device(n_row, n_col, pixels, conv_weight, time_weight, class_weight, *rest):
+    args = (pixels, conv_weight, time_weight.transpose(0, 2, 3, 1), class_weight.T, *rest)
     n_a = 2 * n_col
     n_b = n_row // 2
     rows = CONV_ROWS + SMALL_ROWS
@@ -582,17 +637,21 @@
     total = shard * n_a
     vmem = pl.BlockSpec(memory_space=pltpu.VMEM)
     dma = pltpu.SemaphoreType.DMA
-    return pl.pallas_call(
+    anywhere = pl.BlockSpec(memory_space=pl.ANY)
+    gx, final = pl.pallas_call(
         functools.partial(kernel, n_row, n_col, shard),
         out_shape=(
             jax.ShapeDtypeStruct((T, T, LX), BF16),
-            jax.ShapeDtypeStruct((3, 3, C_IN, C_OUT), F32),
-            jax.ShapeDtypeStruct((3, GROUPS, CPG, CPG), F32),
-            jax.ShapeDtypeStruct((C_OUT, CLASSES), F32),
+            jax.ShapeDtypeStruct((total, 128), BF16),
         ),
-        in_specs=[vmem] * 8,
-        out_specs=(vmem,) * 4,
+        in_specs=[anywhere] * 8,
+        out_specs=(anywhere,) * 2,
         scratch_shapes=[
+            pltpu.VMEM((T, T, LX), BF16),
+            pltpu.VMEM((total, 128), BF16),
+            dma((2,)),
+            *[pltpu.VMEM(arg.shape, arg.dtype) for arg in args],
+            dma((8,)),
             pltpu.VMEM((PAIRS, PIX, 128), F32),
             pltpu.VMEM((2, PAIRS, PIX + 2 * T, 128), F32),
             pltpu.VMEM((3, T + 2, T, LX), BF16),
@@ -623,7 +682,6 @@
             pltpu.VMEM((total, 128), BF16),
             pltpu.VMEM((n_a, shard, 128), BF16),
             pltpu.VMEM((n_b, shard, 128), BF16),
-            pltpu.VMEM((total, 128), BF16),
             dma((9,)),
             dma((9,)),
             dma((9,)),
@@ -642,9 +700,23 @@
             dma((n_a,)),
         ],
         compiler_params=pltpu.CompilerParams(
-            collective_id=0, has_side_effects=True, vmem_limit_bytes=40 * 1024 * 1024
+            collective_id=0, has_side_effects=True, vmem_limit_bytes=VMEM_GRANT
         ),
     )(*args)
+    gx, conv_grad, time_grad, class_grad = pl.pallas_call(
+        finish,
+        out_shape=(
+            jax.ShapeDtypeStruct((T, T, LX), BF16),
+            jax.ShapeDtypeStruct((3, 3, C_IN, C_OUT), F32),
+            jax.ShapeDtypeStruct((3, CPG, CPG, GROUPS), F32),
+            jax.ShapeDtypeStruct((CLASSES, C_OUT), F32),
+        ),
+        in_specs=[anywhere, vmem],
+        out_specs=(anywhere, vmem, vmem, vmem),
+        scratch_shapes=[dma],
+        compiler_params=pltpu.CompilerParams(vmem_limit_bytes=VMEM_GRANT),
+    )(gx, final)
+    return gx, conv_grad, time_grad.transpose(0, 3, 1, 2), class_grad.T
 
 
 def solution(mesh):

time: 40.5 us -> 49.6 us (1.22)
  Pallas kernels: 33.9 us -> 48.8 us
  local copies, waits for them, and re-layouts: 5.72 us -> 0 us
    pallas_call x0 -> x1, Pallas kernels: none -> 14.7 us  [per_device(): pl.pallas_call(finish, out_shape=(jax.ShapeDtypeStruct((T, T, LX), BF16),...]
    unnamed x16 -> x0, local copies, waits for them, and re-layouts: 4.27 us -> none
    pallas_call x2 -> x0, local copies, waits for them, and re-layouts: 1.44 us -> none  [per_device(): pl.pallas_call(functools.partial(kernel, n_row, n_col, shard), out_shape=...]
where the time goes in v2:
time: 49.6 us; the launch traced here: 49.4 us
  Pallas kernels  48.8 us (98%)
  between operations  0.64 us (1%)
    pallas_call x1, Pallas kernels, per_device(): pl.pallas_call(functools.partial(kernel, n_row, n_col, shard), out_shape=...  34.1 us
    pallas_call x1, Pallas kernels, per_device(): pl.pallas_call(finish, out_shape=(jax.ShapeDtypeStruct((T, T, LX), BF16),...  14.7 us

profile of v2, /device:TPU:0, one launch (start us, length us, event | category | flops | bytes accessed | tf_op | source)
XLA Modules:
  0.0 49.4 jit_solution(3071233569240496110)
XLA Ops:
  0.6 34.1 %shard_map.111 = (bf16[16,16,768]{2,1,0:T(8,128)(2,1)}, bf16[640,128]{1,0:T(8,128)(2,1)}) custom-call(bf16[16,16,768]{2,1,0:T(8,128)(2,1)} %x_hbm.1, bf16[3,3,64,128]{3,2,1,0:T(8,128)(2,1)} %cw_hbm.1, bf16[3,8,8,16]{3,2,1,0:T(8,128)(2,1)} %bitcast.4, bf16[20,128]{1,0:T(8,128)(2,1)} %bitcast.5, s32[16,16]{1,0:T(8,128)} %slot_hbm.1, s32[1,1,32]{2,1,0:T(1,128)} %sdir_hbm.1, ...), custom_call_target="tpu_custom_call" | custom-call | tf_op jit(solution)/shard_map/pallas_call | solution.py:641
  34.7 14.7 %shard_map.112 = (bf16[16,16,768]{2,1,0:T(8,128)(2,1)}, f32[3,3,64,128]{3,2,1,0:T(8,128)}, f32[3,8,8,16]{3,2,1,0:T(8,128)}, f32[20,128]{1,0:T(8,128)}) custom-call(bf16[16,16,768]{2,1,0:T(8,128)(2,1)} %get-tuple-element.10.gx_in, bf16[640,128]{1,0:T(8,128)(2,1)} %get-tuple-element.11.final), custom_call_target="tpu_custom_call" | custom-call | tf_op jit(solution)/shard_map/pallas_call | solution.py:706

commit v3 on v2

--- a/solution.py
+++ b/solution.py
@@ -22,6 +22,7 @@
 BF16 = jnp.bfloat16
 
 VMEM_GRANT = 63 * 1024 * 1024
+CHUNKS = 4
 T = 16
 PIX = T * T
 PAIRS = DATES // 2
@@ -609,11 +610,33 @@
     final_store.wait()
 
 
-def finish(gx_in, final, gx_out, gcw_ref, gtw_ref, gkw_ref, sem):
-    copy = pltpu.make_async_copy(gx_in, gx_out, sem)
-    copy.start()
+def finish(
+    gx_in, final_in, gx_out, gcw_out, gtw_out, gkw_out,
+    held, final, gcw_ref, gtw_ref, gkw_ref, in_sems, out_sems,
+):
+    rows = T // CHUNKS
+    parts = [pl.ds(i * rows, rows) for i in range(CHUNKS)]
+    loads = [
+        pltpu.make_async_copy(gx_in.at[at], held.at[at], in_sems.at[i])
+        for i, at in enumerate(parts)
+    ]
+    stores = [
+        pltpu.make_async_copy(held.at[at], gx_out.at[at], out_sems.at[i])
+        for i, at in enumerate(parts)
+    ]
+    for i, (src, dst) in enumerate(((gcw_ref, gcw_out), (gtw_ref, gtw_out), (gkw_ref, gkw_out))):
+        stores.append(pltpu.make_async_copy(src, dst, out_sems.at[CHUNKS + i]))
+    final_load = pltpu.make_async_copy(final_in, final, in_sems.at[CHUNKS])
+    final_load.start()
+    for load in loads:
+        load.start()
+    final_load.wait()
     for t in range(9):
         gcw_ref[t // 3, t % 3] = final[t * 64 : (t + 1) * 64, :].astype(F32)
+    stores[CHUNKS].start()
+    for load, store in zip(loads, stores):
+        load.wait()
+        store.start()
     width = 3 * CPG * CPG
     small = final[CONV_ROWS : CONV_ROWS + SMALL_ROWS, :]
     repeat = (lax.div(iota((width, SMALL_ROWS), 0), CPG) == iota((width, SMALL_ROWS), 1)).astype(
@@ -625,7 +648,10 @@
     rows = jnp.where(own_out, rows, 0.0).astype(BF16)
     gtw_ref[...] = dot(rows, fold).reshape(3, CPG, CPG, GROUPS)
     gkw_ref[...] = small[3 * CPG : 3 * CPG + CLASSES].astype(F32)
-    copy.wait()
+    stores[CHUNKS + 1].start()
+    stores[CHUNKS + 2].start()
+    for store in stores:
+        store.wait()
 
 
 def per_device(n_row, n_col, pixels, conv_weight, time_weight, class_weight, *rest):
@@ -635,7 +661,6 @@
     rows = CONV_ROWS + SMALL_ROWS
     shard = -(-rows // (16 * n_a)) * 16
     total = shard * n_a
-    vmem = pl.BlockSpec(memory_space=pltpu.VMEM)
     dma = pltpu.SemaphoreType.DMA
     anywhere = pl.BlockSpec(memory_space=pl.ANY)
     gx, final = pl.pallas_call(
@@ -711,9 +736,17 @@
             jax.ShapeDtypeStruct((3, CPG, CPG, GROUPS), F32),
             jax.ShapeDtypeStruct((CLASSES, C_OUT), F32),
         ),
-        in_specs=[anywhere, vmem],
-        out_specs=(anywhere, vmem, vmem, vmem),
-        scratch_shapes=[dma],
+        in_specs=[anywhere] * 2,
+        out_specs=(anywhere,) * 4,
+        scratch_shapes=[
+            pltpu.VMEM((T, T, LX), BF16),
+            pltpu.VMEM((total, 128), BF16),
+            pltpu.VMEM((3, 3, C_IN, C_OUT), F32),
+            pltpu.VMEM((3, CPG, CPG, GROUPS), F32),
+            pltpu.VMEM((CLASSES, C_OUT), F32),
+            dma((CHUNKS + 1,)),
+            dma((CHUNKS + 3,)),
+        ],
         compiler_params=pltpu.CompilerParams(vmem_limit_bytes=VMEM_GRANT),
     )(gx, final)
     return gx, conv_grad, time_grad.transpose(0, 3, 1, 2), class_grad.T

time: 49.6 us -> 37 us (0.75)
  Pallas kernels: 48.8 us -> 36.2 us
    pallas_call x1, Pallas kernels: 14.7 us -> 2.13 us  [per_device(): pl.pallas_call(finish, out_shape=(jax.ShapeDtypeStruct((T, T, LX), BF16),...]
where the time goes in v3:
time: 37 us; the launch traced here: 36.9 us
  Pallas kernels  36.2 us (98%)
  between operations  0.64 us (2%)
    pallas_call x1, Pallas kernels, per_device(): pl.pallas_call(functools.partial(kernel, n_row, n_col, shard), out_shape=...  34.1 us
    pallas_call x1, Pallas kernels, per_device(): pl.pallas_call(finish, out_shape=(jax.ShapeDtypeStruct((T, T, LX), BF16),...  2.13 us

profile of v3, /device:TPU:0, one launch (start us, length us, event | category | flops | bytes accessed | tf_op | source)
XLA Modules:
  0.0 36.9 jit_solution(6490973258898522008)
XLA Ops:
  0.6 34.1 %shard_map.111 = (bf16[16,16,768]{2,1,0:T(8,128)(2,1)}, bf16[640,128]{1,0:T(8,128)(2,1)}) custom-call(bf16[16,16,768]{2,1,0:T(8,128)(2,1)} %x_hbm.1, bf16[3,3,64,128]{3,2,1,0:T(8,128)(2,1)} %cw_hbm.1, bf16[3,8,8,16]{3,2,1,0:T(8,128)(2,1)} %bitcast.4, bf16[20,128]{1,0:T(8,128)(2,1)} %bitcast.5, s32[16,16]{1,0:T(8,128)} %slot_hbm.1, s32[1,1,32]{2,1,0:T(1,128)} %sdir_hbm.1, ...), custom_call_target="tpu_custom_call" | custom-call | tf_op jit(solution)/shard_map/pallas_call | solution.py:666
  34.7 2.1 %shard_map.112 = (bf16[16,16,768]{2,1,0:T(8,128)(2,1)}, f32[3,3,64,128]{3,2,1,0:T(8,128)}, f32[3,8,8,16]{3,2,1,0:T(8,128)}, f32[20,128]{1,0:T(8,128)}) custom-call(bf16[16,16,768]{2,1,0:T(8,128)(2,1)} %get-tuple-element.10.gx_in, bf16[640,128]{1,0:T(8,128)(2,1)} %get-tuple-element.11.final_in), custom_call_target="tpu_custom_call" | custom-call | tf_op jit(solution)/shard_map/pallas_call | solution.py:731

commit v4 on v3

--- a/solution.py
+++ b/solution.py
@@ -452,11 +452,14 @@
         gpre[1 : T + 1, :, p * 256 : (p + 1) * 256] = g_pre.reshape(T, T, 256)
     start_all(row_copy, (1, 7))
 
-    conv_t = None
-    for p in range(PAIRS):
-        g_pair = gpre[1 : T + 1, :, p * 256 : (p + 1) * 256].reshape(PIX, 256)
-        term = dot(g_pair, taps(p), ((0,), (0,)))
-        conv_t = term if conv_t is None else conv_t + term
+    g_all = jnp.concatenate(
+        [
+            gpre[1 : T + 1, :, p * 256 : (p + 1) * 256].reshape(PIX, 256)
+            for p in range(PAIRS)
+        ],
+        axis=0,
+    )
+    conv_t = dot(g_all, jnp.concatenate([taps(p) for p in range(PAIRS)], axis=0), ((0,), (0,)))
     low_half = iota((128, 128), 1) < C_IN
     for t in range(9):
         both = jnp.where(

time: 37 us -> 37 us (level)
  no operation moved by 1% of the time
where the time goes in v4:
time: 37 us; the launch traced here: 36.9 us
  Pallas kernels  36.2 us (98%)
  between operations  0.64 us (2%)
    pallas_call x1, Pallas kernels, per_device(): pl.pallas_call(functools.partial(kernel, n_row, n_col, shard), out_shape=...  34.1 us
    pallas_call x1, Pallas kernels, per_device(): pl.pallas_call(finish, out_shape=(jax.ShapeDtypeStruct((T, T, LX), BF16),...  2.13 us

profile of v4, /device:TPU:0, one launch (start us, length us, event | category | flops | bytes accessed | tf_op | source)
XLA Modules:
  0.0 36.9 jit_solution(10877119407335001232)
XLA Ops:
  0.6 34.1 %shard_map.111 = (bf16[16,16,768]{2,1,0:T(8,128)(2,1)}, bf16[640,128]{1,0:T(8,128)(2,1)}) custom-call(bf16[16,16,768]{2,1,0:T(8,128)(2,1)} %x_hbm.1, bf16[3,3,64,128]{3,2,1,0:T(8,128)(2,1)} %cw_hbm.1, bf16[3,8,8,16]{3,2,1,0:T(8,128)(2,1)} %bitcast.4, bf16[20,128]{1,0:T(8,128)(2,1)} %bitcast.5, s32[16,16]{1,0:T(8,128)} %slot_hbm.1, s32[1,1,32]{2,1,0:T(1,128)} %sdir_hbm.1, ...), custom_call_target="tpu_custom_call" | custom-call | tf_op jit(solution)/shard_map/pallas_call | solution.py:669
  34.7 2.1 %shard_map.112 = (bf16[16,16,768]{2,1,0:T(8,128)(2,1)}, f32[3,3,64,128]{3,2,1,0:T(8,128)}, f32[3,8,8,16]{3,2,1,0:T(8,128)}, f32[20,128]{1,0:T(8,128)}) custom-call(bf16[16,16,768]{2,1,0:T(8,128)(2,1)} %get-tuple-element.10.gx_in, bf16[640,128]{1,0:T(8,128)(2,1)} %get-tuple-element.11.final_in), custom_call_target="tpu_custom_call" | custom-call | tf_op jit(solution)/shard_map/pallas_call | solution.py:734
